TPU v7x, 256 devices: a whole 4x4x8 slice. The times are simulated.
256 devices in a mesh: strike: 32 (over z, y_hi, core), cross: 8 (over x, y_lo).
Axes of the slice: x: 4, y: 4 (y_hi: 2, y_lo: 2; y = y_hi * 2 + y_lo), z: 8, core: 2. Of those that a mesh axis runs over, the one named last changes fastest.
Arguments:
- velocity: float32 [3, 512, 128, 256], P(None, 'strike', 'cross'), may hold values from -4 to 4
- stress: float32 [6, 512, 128, 256], P(None, 'strike', 'cross'), may hold values from -1.6 to 1.6
- buoyancy: float32 [512, 128, 256], P('strike', 'cross'), may hold values from 0.5 to 1
- lame: float32 [512, 128, 256], P('strike', 'cross'), may hold values from 0.5 to 1.2
- shear: float32 [512, 128, 256], P('strike', 'cross'), may hold values from 0.5 to 1
- fault_tile: int32 [32], replicated, may hold values from 1 to 7
- prestress: float32 [512, 256], P('strike', 'cross'), may hold values from 1.2 to 2.4
- normal_stress: float32 [512, 256], P('strike', 'cross'), may hold values from 2 to 4
- rate_a: float32 [512, 256], P('strike', 'cross'), may hold values from 0.02 to 0.04
- state: float32 [512, 256], P('strike', 'cross'), may hold values from 0.45 to 0.6
Outputs:
- velocity_out: float32 [3, 512, 128, 256], P(None, 'strike', 'cross')
- stress_out: float32 [6, 512, 128, 256], P(None, 'strike', 'cross')
- slip_rate: float32 [512, 256], P('strike', 'cross')
- state_out: float32 [512, 256], P('strike', 'cross')
Inputs may be any that keep to these rules, and one draw needn't show every extreme that they name: `fault_tile`: each strike index has its fault plane in the first row of one cross tile other than the first.
All inputs are finite; a program needn't handle non-finite values.
Results may differ from a plain program's by a relative error of at most 0.0003.
Values sent between devices are 32-bit elements; how exact they have to be, the bound alone decides.
A program may use at most 64 MiB of HBM per device.

v0:
```python
import jax
import jax.numpy as jnp
from jax import lax
from jax.sharding import PartitionSpec as P

STEPS = 4
NEWTON = 8
step_ratio = 0.25
ref_rate = 0.001
evolve_rate = 1e-05
base_friction = 0.6
evolve_b = 0.03


def with_halo(shard, sides, width):
    for axis, dim in sides:
        size, length = (lax.axis_size(axis), shard.shape[dim])
        up = [(i, (i + 1) % size) for i in range(size - 1)]
        down = [(j, i) for i, j in up]
        last = lax.slice_in_dim(shard, length - width, length, axis=dim)
        first = lax.slice_in_dim(shard, 0, width, axis=dim)
        before = lax.ppermute(last, axis, up)
        after = lax.ppermute(first, axis, down)
        shard = jnp.concatenate([before, shard, after], axis=dim)
    return shard


def inverse_sinh(value):
    magnitude = jnp.abs(value)
    return jnp.sign(value) * jnp.log(magnitude + jnp.sqrt(magnitude * magnitude + 1.0))


def shifted(field, axis_pos, offset):
    parts = [slice(2, field.shape[position] - 2) for position in range(3)]
    parts[axis_pos] = slice(2 + offset, field.shape[axis_pos] - 2 + offset)
    return field[tuple(parts)]


def forward_diff(field, axis_pos):
    return (
        1.125 * (shifted(field, axis_pos, 1) - shifted(field, axis_pos, 0))
        - (shifted(field, axis_pos, 2) - shifted(field, axis_pos, -1)) / 24.0
    )


def backward_diff(field, axis_pos):
    return (
        1.125 * (shifted(field, axis_pos, 0) - shifted(field, axis_pos, -1))
        - (shifted(field, axis_pos, 1) - shifted(field, axis_pos, -2)) / 24.0
    )


def velocity_update(velocity, padded, buoyancy):
    strike_force = (
        forward_diff(padded[0], 0) + backward_diff(padded[3], 1) + backward_diff(padded[4], 2)
    )
    cross_force = (
        backward_diff(padded[3], 0) + forward_diff(padded[1], 1) + backward_diff(padded[5], 2)
    )
    depth_force = (
        backward_diff(padded[4], 0) + backward_diff(padded[5], 1) + forward_diff(padded[2], 2)
    )
    return velocity + step_ratio * buoyancy * jnp.stack([strike_force, cross_force, depth_force])


def stress_update(stress, padded, lame, shear):
    stretch_strike = backward_diff(padded[0], 0)
    stretch_cross = backward_diff(padded[1], 1)
    stretch_depth = backward_diff(padded[2], 2)
    dilation = stretch_strike + stretch_cross + stretch_depth
    normal = jnp.stack(
        [
            lame * dilation + 2.0 * shear * stretch_strike,
            lame * dilation + 2.0 * shear * stretch_cross,
            lame * dilation + 2.0 * shear * stretch_depth,
        ]
    )
    tangent = shear * jnp.stack(
        [
            forward_diff(padded[0], 1) + forward_diff(padded[1], 0),
            forward_diff(padded[0], 2) + forward_diff(padded[2], 0),
            forward_diff(padded[1], 2) + forward_diff(padded[2], 1),
        ]
    )
    return stress + step_ratio * jnp.concatenate([normal, tangent], 0)


def friction(trial, damping, prestress, normal_stress, rate_a, state):
    total = trial + prestress
    width = 2.0 * ref_rate * jnp.exp(-state / rate_a)
    strength = rate_a * normal_stress
    scaled = inverse_sinh(total / (damping * width))
    for iteration in range(NEWTON):
        residual = strength * scaled + damping * width * jnp.sinh(scaled) - total
        slope = strength + damping * width * jnp.cosh(scaled)
        scaled = scaled - residual / slope
    slip = width * jnp.sinh(scaled)
    traction = total - damping * slip
    evolved = state + evolve_rate * (
        jnp.exp((base_friction - state) / evolve_b) - jnp.abs(slip) / ref_rate
    )
    return (traction - prestress, slip, evolved)


def pad_depth(field):
    return jnp.pad(field, ((0, 0), (0, 0), (0, 0), (2, 2)))


def local(
    velocity, stress, buoyancy, lame, shear, fault_tile, prestress, normal_stress, rate_a, state
):
    strike_pos = lax.axis_index("strike")
    cross_pos = lax.axis_index("cross")
    is_owner = fault_tile[strike_pos] == cross_pos
    damping = 0.5 * jnp.sqrt(shear[:, 0, :] / buoyancy[:, 0, :])
    fault_prestress, fault_normal, fault_rate, fault_state = (
        lax.all_gather(prestress, "cross", axis=1, tiled=True),
        lax.all_gather(normal_stress, "cross", axis=1, tiled=True),
        lax.all_gather(rate_a, "cross", axis=1, tiled=True),
        lax.all_gather(state, "cross", axis=1, tiled=True),
    )
    slip = jnp.zeros_like(fault_state)
    for iteration in range(STEPS):
        stress_wide = with_halo(stress, (("strike", 1), ("cross", 2)), 2)
        velocity = velocity_update(velocity, pad_depth(stress_wide), buoyancy)
        velocity_wide = with_halo(velocity, (("strike", 1), ("cross", 2)), 2)
        stress = stress_update(stress, pad_depth(velocity_wide), lame, shear)
        trial = stress[3, :, 0, :]
        change, slip, fault_state = friction(
            trial, damping, fault_prestress, fault_normal, fault_rate, fault_state
        )
        update = jnp.where(is_owner, change, trial)
        stress = stress.at[3, :, 0, :].set(update)
    slip_out, state_out = (
        lax.psum_scatter(jnp.where(is_owner, slip, 0.0), "cross", scatter_dimension=1, tiled=True),
        lax.psum_scatter(
            jnp.where(is_owner, fault_state, 0.0), "cross", scatter_dimension=1, tiled=True
        ),
    )
    return (velocity, stress, slip_out, state_out)


def solution(mesh):
    in_specs = (
        P(None, "strike", "cross", None),
        P(None, "strike", "cross", None),
        P("strike", "cross", None),
        P("strike", "cross", None),
        P("strike", "cross", None),
        P(),
        P("strike", "cross"),
        P("strike", "cross"),
        P("strike", "cross"),
        P("strike", "cross"),
    )
    out_specs = (
        P(None, "strike", "cross", None),
        P(None, "strike", "cross", None),
        P("strike", "cross"),
        P("strike", "cross"),
    )
    return jax.shard_map(local, mesh=mesh, in_specs=in_specs, out_specs=out_specs, check_vma=False)
```

profile of v0, /device:TPU:32, one launch (start us, length us, event | category | flops | bytes accessed | tf_op | source)
XLA Modules:
  0.0 468.4 jit_solution(657342428143192859)
XLA Ops:
  7.2 2.3 copy.51
  9.7 1.9 collective-permute-start
  11.6 6.0 %collective-permute-start.1 = (f32[6,2,16,256]{3,1,2,0:T(2,128)S(1)}, f32[6,2,16,256]{3,1,2,0:T(2,128)S(1)}, u32[]{:S(2)}, u32[]{:S(2)}) collective-permute-start(f32[6,2,16,256]{3,1,2,0:T(2,128)S(1)} %get-tuple-element.137), channel_id=1, source_target_pairs={{8,0},{16,8},{24,16},{32,24},{40,32},{48,40},{56,48},{64,56},{72,6... | collective-permute-start | bytes 589832 | tf_op jit(solution)/shard_map/ppermute | solution.py:23
  17.7 1.4 collective-permute-done
  19.1 1.8 collective-permute-done.1
  20.9 3.5 collective-permute-start.2
  24.5 1.3 collective-permute-start.3
  26.0 11.5 %collective-permute-done.2 = f32[6,20,2,256]{3,1,2,0:T(8,128)S(1)} collective-permute-done((f32[6,20,2,256]{3,1,2,0:T(8,128)S(1)}, f32[6,20,2,256]{3,1,2,0:T(8,128)S(1)}, u32[]{:S(2)}, u32[]{:S(2)}) %collective-permute-start.2) | collective-permute-done | bytes 245792 | tf_op jit(solution)/shard_map/ppermute | solution.py:22
  37.5 3.0 select_maximum_fusion.12
  44.1 2.7 collective-permute-start.4
  46.8 5.3 %collective-permute-start.5 = (f32[3,2,16,256]{3,1,2,0:T(2,128)S(1)}, f32[3,2,16,256]{3,1,2,0:T(2,128)S(1)}, u32[]{:S(2)}, u32[]{:S(2)}) collective-permute-start(f32[3,2,16,256]{3,1,2,0:T(2,128)S(1)} %get-tuple-element.157), channel_id=1, source_target_pairs={{8,0},{16,8},{24,16},{32,24},{40,32},{48,40},{56,48},{64,56},{72,6... | collective-permute-start | bytes 294920 | tf_op jit(solution)/shard_map/ppermute | solution.py:23
  52.5 1.8 collective-permute-done.5
  54.3 4.4 collective-permute-start.6
  58.7 1.3 collective-permute-start.7
  60.1 31.8 %all-gather = f32[8,32,16]{1,2,0:T(8,128)S(1)} all-gather(f32[1,32,16]{1,2,0:T(8,128)S(1)} %bitcast.312), channel_id=1, replica_groups=mesh['strike'=32,'cross'=8] {'cross'}, dimensions={0}, use_global_device_ids=true | all-gather | bytes 18432 | tf_op jit(solution)/shard_map/all_gather | solution.py:117
  92.0 28.2 %all-gather.3 = f32[8,32,16]{1,2,0:T(8,128)S(1)} all-gather(f32[1,32,16]{1,2,0:T(8,128)S(1)} %bitcast.313), channel_id=1, replica_groups=mesh['strike'=32,'cross'=8] {'cross'}, dimensions={0}, use_global_device_ids=true | all-gather | bytes 18432 | tf_op jit(solution)/shard_map/all_gather | solution.py:118
  120.2 28.2 %all-gather.2 = f32[8,32,16]{1,2,0:T(8,128)S(1)} all-gather(f32[1,32,16]{1,2,0:T(8,128)S(1)} %bitcast.314), channel_id=1, replica_groups=mesh['strike'=32,'cross'=8] {'cross'}, dimensions={0}, use_global_device_ids=true | all-gather | bytes 18432 | tf_op jit(solution)/shard_map/all_gather | solution.py:119
  148.5 28.3 %all-gather.1 = f32[8,32,16]{1,2,0:T(8,128)S(1)} all-gather(f32[1,32,16]{1,2,0:T(8,128)S(1)} %bitcast.315), channel_id=1, replica_groups=mesh['strike'=32,'cross'=8] {'cross'}, dimensions={0}, use_global_device_ids=true | all-gather | bytes 18432 | tf_op jit(solution)/shard_map/all_gather | solution.py:120
  185.6 1.9 collective-permute-start.8
  187.5 6.0 %collective-permute-start.9 = (f32[6,2,16,256]{3,1,2,0:T(2,128)S(1)}, f32[6,2,16,256]{3,1,2,0:T(2,128)S(1)}, u32[]{:S(2)}, u32[]{:S(2)}) collective-permute-start(f32[6,2,16,256]{3,1,2,0:T(2,128)S(1)} %get-tuple-element.135), channel_id=1, source_target_pairs={{8,0},{16,8},{24,16},{32,24},{40,32},{48,40},{56,48},{64,56},{72,6... | collective-permute-start | bytes 589832 | tf_op jit(solution)/shard_map/ppermute | solution.py:23
  193.6 1.4 collective-permute-done.8
  195.0 1.8 collective-permute-done.9
  196.9 1.3 collective-permute-start.10
  198.2 1.3 collective-permute-start.11
  199.5 12.4 %collective-permute-done.10 = f32[6,20,2,256]{3,1,2,0:T(8,128)S(1)} collective-permute-done((f32[6,20,2,256]{3,1,2,0:T(8,128)S(1)}, f32[6,20,2,256]{3,1,2,0:T(8,128)S(1)}, u32[]{:S(2)}, u32[]{:S(2)}) %collective-permute-start.10) | collective-permute-done | bytes 245792 | tf_op jit(solution)/shard_map/ppermute | solution.py:22
  211.9 3.0 select_maximum_fusion.8
  218.3 1.9 collective-permute-start.12
  220.3 6.0 %collective-permute-start.13 = (f32[3,2,16,256]{3,1,2,0:T(2,128)S(1)}, f32[3,2,16,256]{3,1,2,0:T(2,128)S(1)}, u32[]{:S(2)}, u32[]{:S(2)}) collective-permute-start(f32[3,2,16,256]{3,1,2,0:T(2,128)S(1)} %get-tuple-element.155), channel_id=1, source_target_pairs={{8,0},{16,8},{24,16},{32,24},{40,32},{48,40},{56,48},{64,56},{72,6... | collective-permute-start | bytes 294920 | tf_op jit(solution)/shard_map/ppermute | solution.py:23
  226.7 1.8 collective-permute-done.13
  228.6 4.4 collective-permute-start.14
  232.9 1.5 collective-permute-start.15
  235.6 4.4 collective-permute-done.15
  244.8 1.9 collective-permute-start.16
  246.7 6.0 %collective-permute-start.17 = (f32[6,2,16,256]{3,1,2,0:T(2,128)S(1)}, f32[6,2,16,256]{3,1,2,0:T(2,128)S(1)}, u32[]{:S(2)}, u32[]{:S(2)}) collective-permute-start(f32[6,2,16,256]{3,1,2,0:T(2,128)S(1)} %get-tuple-element.133), channel_id=1, source_target_pairs={{8,0},{16,8},{24,16},{32,24},{40,32},{48,40},{56,48},{64,56},{72,6... | collective-permute-start | bytes 589832 | tf_op jit(solution)/shard_map/ppermute | solution.py:23
  252.8 1.4 collective-permute-done.16
  254.2 1.8 collective-permute-done.17
  256.1 4.8 %collective-permute-start.18 = (f32[6,20,2,256]{3,1,2,0:T(8,128)S(1)}, f32[6,20,2,256]{3,1,2,0:T(8,128)S(1)}, u32[]{:S(2)}, u32[]{:S(2)}) collective-permute-start(f32[6,20,2,256]{3,1,2,0:T(8,128)S(1)} %get-tuple-element.124), channel_id=1, source_target_pairs={{0,1},{1,2},{2,3},{3,4},{4,5},{5,6},{6,7},{8,9},{9,10},{10,11},{11... | collective-permute-start | bytes 737288 | tf_op jit(solution)/shard_map/ppermute | solution.py:22
  262.2 11.6 %collective-permute-done.18 = f32[6,20,2,256]{3,1,2,0:T(8,128)S(1)} collective-permute-done((f32[6,20,2,256]{3,1,2,0:T(8,128)S(1)}, f32[6,20,2,256]{3,1,2,0:T(8,128)S(1)}, u32[]{:S(2)}, u32[]{:S(2)}) %collective-permute-start.18) | collective-permute-done | bytes 245792 | tf_op jit(solution)/shard_map/ppermute | solution.py:22
  273.7 3.0 select_maximum_fusion.4
  280.3 1.9 collective-permute-start.20
  282.3 6.0 %collective-permute-start.21 = (f32[3,2,16,256]{3,1,2,0:T(2,128)S(1)}, f32[3,2,16,256]{3,1,2,0:T(2,128)S(1)}, u32[]{:S(2)}, u32[]{:S(2)}) collective-permute-start(f32[3,2,16,256]{3,1,2,0:T(2,128)S(1)} %get-tuple-element.153), channel_id=1, source_target_pairs={{8,0},{16,8},{24,16},{32,24},{40,32},{48,40},{56,48},{64,56},{72,6... | collective-permute-start | bytes 294920 | tf_op jit(solution)/shard_map/ppermute | solution.py:23
  288.7 1.8 collective-permute-done.21
  290.6 4.4 collective-permute-start.22
  295.0 1.7 collective-permute-start.23
  297.6 4.4 collective-permute-done.23
  306.8 1.9 collective-permute-start.24
  308.7 6.0 %collective-permute-start.25 = (f32[6,2,16,256]{3,1,2,0:T(2,128)S(1)}, f32[6,2,16,256]{3,1,2,0:T(2,128)S(1)}, u32[]{:S(2)}, u32[]{:S(2)}) collective-permute-start(f32[6,2,16,256]{3,1,2,0:T(2,128)S(1)} %get-tuple-element.131), channel_id=1, source_target_pairs={{8,0},{16,8},{24,16},{32,24},{40,32},{48,40},{56,48},{64,56},{72,6... | collective-permute-start | bytes 589832 | tf_op jit(solution)/shard_map/ppermute | solution.py:23
  314.8 1.4 collective-permute-done.24
  316.2 1.8 collective-permute-done.25
  318.1 4.8 %collective-permute-start.26 = (f32[6,20,2,256]{3,1,2,0:T(8,128)S(1)}, f32[6,20,2,256]{3,1,2,0:T(8,128)S(1)}, u32[]{:S(2)}, u32[]{:S(2)}) collective-permute-start(f32[6,20,2,256]{3,1,2,0:T(8,128)S(1)} %get-tuple-element.122), channel_id=1, source_target_pairs={{0,1},{1,2},{2,3},{3,4},{4,5},{5,6},{6,7},{8,9},{9,10},{10,11},{11... | collective-permute-start | bytes 737288 | tf_op jit(solution)/shard_map/ppermute | solution.py:22
  324.2 11.6 %collective-permute-done.26 = f32[6,20,2,256]{3,1,2,0:T(8,128)S(1)} collective-permute-done((f32[6,20,2,256]{3,1,2,0:T(8,128)S(1)}, f32[6,20,2,256]{3,1,2,0:T(8,128)S(1)}, u32[]{:S(2)}, u32[]{:S(2)}) %collective-permute-start.26) | collective-permute-done | bytes 245792 | tf_op jit(solution)/shard_map/ppermute | solution.py:22
  335.8 3.0 select_maximum_fusion
  342.4 1.9 collective-permute-start.28
  344.3 6.0 %collective-permute-start.29 = (f32[3,2,16,256]{3,1,2,0:T(2,128)S(1)}, f32[3,2,16,256]{3,1,2,0:T(2,128)S(1)}, u32[]{:S(2)}, u32[]{:S(2)}) collective-permute-start(f32[3,2,16,256]{3,1,2,0:T(2,128)S(1)} %get-tuple-element.151), channel_id=1, source_target_pairs={{8,0},{16,8},{24,16},{32,24},{40,32},{48,40},{56,48},{64,56},{72,6... | collective-permute-start | bytes 294920 | tf_op jit(solution)/shard_map/ppermute | solution.py:23
  350.8 1.8 collective-permute-done.29
  352.6 4.4 collective-permute-start.30
  357.0 1.5 collective-permute-start.31
  358.5 1.3 copy.68
  359.8 4.2 collective-permute-done.31
  370.3 2.0 copy.69
  372.4 46.8 %reduce-scatter.7.cloned.1.call-done = f32[32,16]{1,0:T(8,128)} async-done(((f32[256,16]{1,0:T(8,128)}), f32[32,16]{1,0:T(8,128)}) %reduce-scatter.7.cloned.1.call-update) | async-done | bytes 2064
  419.2 1.4 copy.71
  420.6 39.4 %reduce-scatter.9.cloned.1.call-done = f32[32,16]{1,0:T(8,128)} async-done(((f32[256,16]{1,0:T(8,128)}), f32[32,16]{1,0:T(8,128)}) %reduce-scatter.9.cloned.1.call-update) | async-done | bytes 2064
  460.0 1.4 copy.73
  (132 shorter events, 45.4 us)
Async XLA Ops:
  7.2 412.0 %reduce-scatter.7.cloned.1.call-start = ((), (), s32[]{:S(2)}) async-start(), calls=%async_computation.2 | async-start | bytes 147456
  9.5 16.2 %copy-start.4 = (f32[16,16,256]{2,1,0:T(8,128)S(1)}, f32[16,16,256]{2,1,0:T(8,128)}, u32[]{:S(2)}) copy-start(f32[16,16,256]{2,1,0:T(8,128)} %param.20) | copy-start | bytes 786436
  9.7 9.4 %collective-permute-start = (f32[6,2,16,256]{3,1,2,0:T(2,128)S(1)}, f32[6,2,16,256]{3,1,2,0:T(2,128)S(1)}, u32[]{:S(2)}, u32[]{:S(2)}) collective-permute-start(f32[6,2,16,256]{3,1,2,0:T(2,128)S(1)} %get-tuple-element.136), channel_id=1, source_target_pairs={{0,8},{8,16},{16,24},{24,32},{32,40},{40,48},{48,56},{56,64},{64,7... | collective-permute-start | bytes 589832 | tf_op jit(solution)/shard_map/ppermute | solution.py:22
  11.6 9.2 %collective-permute-start.1 = (f32[6,2,16,256]{3,1,2,0:T(2,128)S(1)}, f32[6,2,16,256]{3,1,2,0:T(2,128)S(1)}, u32[]{:S(2)}, u32[]{:S(2)}) collective-permute-start(f32[6,2,16,256]{3,1,2,0:T(2,128)S(1)} %get-tuple-element.137), channel_id=1, source_target_pairs={{8,0},{16,8},{24,16},{32,24},{40,32},{48,40},{56,48},{64,56},{72,6... | collective-permute-start | bytes 589832 | tf_op jit(solution)/shard_map/ppermute | solution.py:23
  20.9 16.5 %collective-permute-start.2 = (f32[6,20,2,256]{3,1,2,0:T(8,128)S(1)}, f32[6,20,2,256]{3,1,2,0:T(8,128)S(1)}, u32[]{:S(2)}, u32[]{:S(2)}) collective-permute-start(f32[6,20,2,256]{3,1,2,0:T(8,128)S(1)} %get-tuple-element.128), channel_id=1, source_target_pairs={{0,1},{1,2},{2,3},{3,4},{4,5},{5,6},{6,7},{8,9},{9,10},{10,11},{11... | collective-permute-start | bytes 737288 | tf_op jit(solution)/shard_map/ppermute | solution.py:22
  24.5 13.0 %collective-permute-start.3 = (f32[6,20,2,256]{3,1,2,0:T(8,128)S(1)}, f32[6,20,2,256]{3,1,2,0:T(8,128)S(1)}, u32[]{:S(2)}, u32[]{:S(2)}) collective-permute-start(f32[6,20,2,256]{3,1,2,0:T(8,128)S(1)} %get-tuple-element.129), channel_id=1, source_target_pairs={{1,0},{2,1},{3,2},{4,3},{5,4},{6,5},{7,6},{9,8},{10,9},{11,10},{12... | collective-permute-start | bytes 737288 | tf_op jit(solution)/shard_map/ppermute | solution.py:23
  42.4 1.1 copy-start.1
  43.5 16.6 %copy-start.5 = (f32[16,32]{1,0:T(8,128)S(1)}, f32[16,32]{1,0:T(8,128)}, u32[]{:S(2)}) copy-start(f32[16,32]{1,0:T(8,128)} %param.24) | copy-start | bytes 6148
  43.5 48.4 %copy-start.6 = (f32[16,32]{1,0:T(8,128)S(1)}, f32[16,32]{1,0:T(8,128)}, u32[]{:S(2)}) copy-start(f32[16,32]{1,0:T(8,128)} %param.25) | copy-start | bytes 6148
  43.5 76.7 %copy-start.7 = (f32[16,32]{1,0:T(8,128)S(1)}, f32[16,32]{1,0:T(8,128)}, u32[]{:S(2)}) copy-start(f32[16,32]{1,0:T(8,128)} %param.26) | copy-start | bytes 6148
  43.5 105.0 %copy-start.8 = (f32[16,32]{1,0:T(8,128)S(1)}, f32[16,32]{1,0:T(8,128)}, u32[]{:S(2)}) copy-start(f32[16,32]{1,0:T(8,128)} %param.27) | copy-start | bytes 6148
  44.1 8.3 %collective-permute-start.4 = (f32[3,2,16,256]{3,1,2,0:T(2,128)S(1)}, f32[3,2,16,256]{3,1,2,0:T(2,128)S(1)}, u32[]{:S(2)}, u32[]{:S(2)}) collective-permute-start(f32[3,2,16,256]{3,1,2,0:T(2,128)S(1)} %get-tuple-element.156), channel_id=1, source_target_pairs={{0,8},{8,16},{16,24},{24,32},{32,40},{40,48},{48,56},{56,64},{64,7... | collective-permute-start | bytes 294920 | tf_op jit(solution)/shard_map/ppermute | solution.py:22
  46.8 7.5 %collective-permute-start.5 = (f32[3,2,16,256]{3,1,2,0:T(2,128)S(1)}, f32[3,2,16,256]{3,1,2,0:T(2,128)S(1)}, u32[]{:S(2)}, u32[]{:S(2)}) collective-permute-start(f32[3,2,16,256]{3,1,2,0:T(2,128)S(1)} %get-tuple-element.157), channel_id=1, source_target_pairs={{8,0},{16,8},{24,16},{32,24},{40,32},{48,40},{56,48},{64,56},{72,6... | collective-permute-start | bytes 294920 | tf_op jit(solution)/shard_map/ppermute | solution.py:23
  54.3 124.5 %collective-permute-start.6 = (f32[3,20,2,256]{3,1,2,0:T(8,128)S(1)}, f32[3,20,2,256]{3,1,2,0:T(8,128)S(1)}, u32[]{:S(2)}, u32[]{:S(2)}) collective-permute-start(f32[3,20,2,256]{3,1,2,0:T(8,128)S(1)} %get-tuple-element.148), channel_id=1, source_target_pairs={{0,1},{1,2},{2,3},{3,4},{4,5},{5,6},{6,7},{8,9},{9,10},{10,11},{11... | collective-permute-start | bytes 368648 | tf_op jit(solution)/shard_map/ppermute | solution.py:22
  58.7 120.1 %collective-permute-start.7 = (f32[3,20,2,256]{3,1,2,0:T(8,128)S(1)}, f32[3,20,2,256]{3,1,2,0:T(8,128)S(1)}, u32[]{:S(2)}, u32[]{:S(2)}) collective-permute-start(f32[3,20,2,256]{3,1,2,0:T(8,128)S(1)} %get-tuple-element.149), channel_id=1, source_target_pairs={{1,0},{2,1},{3,2},{4,3},{5,4},{6,5},{7,6},{9,8},{10,9},{11,10},{12... | collective-permute-start | bytes 368648 | tf_op jit(solution)/shard_map/ppermute | solution.py:23
  180.7 1.0 copy-start
  180.7 1.0 copy-start.3
  182.7 1.4 copy-start.2
  185.6 9.4 %collective-permute-start.8 = (f32[6,2,16,256]{3,1,2,0:T(2,128)S(1)}, f32[6,2,16,256]{3,1,2,0:T(2,128)S(1)}, u32[]{:S(2)}, u32[]{:S(2)}) collective-permute-start(f32[6,2,16,256]{3,1,2,0:T(2,128)S(1)} %get-tuple-element.134), channel_id=1, source_target_pairs={{0,8},{8,16},{16,24},{24,32},{32,40},{40,48},{48,56},{56,64},{64,7... | collective-permute-start | bytes 589832 | tf_op jit(solution)/shard_map/ppermute | solution.py:22
  187.5 9.3 %collective-permute-start.9 = (f32[6,2,16,256]{3,1,2,0:T(2,128)S(1)}, f32[6,2,16,256]{3,1,2,0:T(2,128)S(1)}, u32[]{:S(2)}, u32[]{:S(2)}) collective-permute-start(f32[6,2,16,256]{3,1,2,0:T(2,128)S(1)} %get-tuple-element.135), channel_id=1, source_target_pairs={{8,0},{16,8},{24,16},{32,24},{40,32},{48,40},{56,48},{64,56},{72,6... | collective-permute-start | bytes 589832 | tf_op jit(solution)/shard_map/ppermute | solution.py:23
  196.9 15.0 %collective-permute-start.10 = (f32[6,20,2,256]{3,1,2,0:T(8,128)S(1)}, f32[6,20,2,256]{3,1,2,0:T(8,128)S(1)}, u32[]{:S(2)}, u32[]{:S(2)}) collective-permute-start(f32[6,20,2,256]{3,1,2,0:T(8,128)S(1)} %get-tuple-element.126), channel_id=1, source_target_pairs={{0,1},{1,2},{2,3},{3,4},{4,5},{5,6},{6,7},{8,9},{9,10},{10,11},{11... | collective-permute-start | bytes 737288 | tf_op jit(solution)/shard_map/ppermute | solution.py:22
  198.2 13.7 %collective-permute-start.11 = (f32[6,20,2,256]{3,1,2,0:T(8,128)S(1)}, f32[6,20,2,256]{3,1,2,0:T(8,128)S(1)}, u32[]{:S(2)}, u32[]{:S(2)}) collective-permute-start(f32[6,20,2,256]{3,1,2,0:T(8,128)S(1)} %get-tuple-element.127), channel_id=1, source_target_pairs={{1,0},{2,1},{3,2},{4,3},{5,4},{6,5},{7,6},{9,8},{10,9},{11,10},{12... | collective-permute-start | bytes 737288 | tf_op jit(solution)/shard_map/ppermute | solution.py:23
  218.3 8.3 %collective-permute-start.12 = (f32[3,2,16,256]{3,1,2,0:T(2,128)S(1)}, f32[3,2,16,256]{3,1,2,0:T(2,128)S(1)}, u32[]{:S(2)}, u32[]{:S(2)}) collective-permute-start(f32[3,2,16,256]{3,1,2,0:T(2,128)S(1)} %get-tuple-element.154), channel_id=1, source_target_pairs={{0,8},{8,16},{16,24},{24,32},{32,40},{40,48},{48,56},{56,64},{64,7... | collective-permute-start | bytes 294920 | tf_op jit(solution)/shard_map/ppermute | solution.py:22
  220.3 8.2 %collective-permute-start.13 = (f32[3,2,16,256]{3,1,2,0:T(2,128)S(1)}, f32[3,2,16,256]{3,1,2,0:T(2,128)S(1)}, u32[]{:S(2)}, u32[]{:S(2)}) collective-permute-start(f32[3,2,16,256]{3,1,2,0:T(2,128)S(1)} %get-tuple-element.155), channel_id=1, source_target_pairs={{8,0},{16,8},{24,16},{32,24},{40,32},{48,40},{56,48},{64,56},{72,6... | collective-permute-start | bytes 294920 | tf_op jit(solution)/shard_map/ppermute | solution.py:23
  228.6 7.0 %collective-permute-start.14 = (f32[3,20,2,256]{3,1,2,0:T(8,128)S(1)}, f32[3,20,2,256]{3,1,2,0:T(8,128)S(1)}, u32[]{:S(2)}, u32[]{:S(2)}) collective-permute-start(f32[3,20,2,256]{3,1,2,0:T(8,128)S(1)} %get-tuple-element.146), channel_id=1, source_target_pairs={{0,1},{1,2},{2,3},{3,4},{4,5},{5,6},{6,7},{8,9},{9,10},{10,11},{11... | collective-permute-start | bytes 368648 | tf_op jit(solution)/shard_map/ppermute | solution.py:22
  232.9 7.1 %collective-permute-start.15 = (f32[3,20,2,256]{3,1,2,0:T(8,128)S(1)}, f32[3,20,2,256]{3,1,2,0:T(8,128)S(1)}, u32[]{:S(2)}, u32[]{:S(2)}) collective-permute-start(f32[3,20,2,256]{3,1,2,0:T(8,128)S(1)} %get-tuple-element.147), channel_id=1, source_target_pairs={{1,0},{2,1},{3,2},{4,3},{5,4},{6,5},{7,6},{9,8},{10,9},{11,10},{12... | collective-permute-start | bytes 368648 | tf_op jit(solution)/shard_map/ppermute | solution.py:23
  244.8 9.4 %collective-permute-start.16 = (f32[6,2,16,256]{3,1,2,0:T(2,128)S(1)}, f32[6,2,16,256]{3,1,2,0:T(2,128)S(1)}, u32[]{:S(2)}, u32[]{:S(2)}) collective-permute-start(f32[6,2,16,256]{3,1,2,0:T(2,128)S(1)} %get-tuple-element.132), channel_id=1, source_target_pairs={{0,8},{8,16},{16,24},{24,32},{32,40},{40,48},{48,56},{56,64},{64,7... | collective-permute-start | bytes 589832 | tf_op jit(solution)/shard_map/ppermute | solution.py:22
  246.7 9.3 %collective-permute-start.17 = (f32[6,2,16,256]{3,1,2,0:T(2,128)S(1)}, f32[6,2,16,256]{3,1,2,0:T(2,128)S(1)}, u32[]{:S(2)}, u32[]{:S(2)}) collective-permute-start(f32[6,2,16,256]{3,1,2,0:T(2,128)S(1)} %get-tuple-element.133), channel_id=1, source_target_pairs={{8,0},{16,8},{24,16},{32,24},{40,32},{48,40},{56,48},{64,56},{72,6... | collective-permute-start | bytes 589832 | tf_op jit(solution)/shard_map/ppermute | solution.py:23
  256.1 17.7 %collective-permute-start.18 = (f32[6,20,2,256]{3,1,2,0:T(8,128)S(1)}, f32[6,20,2,256]{3,1,2,0:T(8,128)S(1)}, u32[]{:S(2)}, u32[]{:S(2)}) collective-permute-start(f32[6,20,2,256]{3,1,2,0:T(8,128)S(1)} %get-tuple-element.124), channel_id=1, source_target_pairs={{0,1},{1,2},{2,3},{3,4},{4,5},{5,6},{6,7},{8,9},{9,10},{10,11},{11... | collective-permute-start | bytes 737288 | tf_op jit(solution)/shard_map/ppermute | solution.py:22
  260.9 12.9 %collective-permute-start.19 = (f32[6,20,2,256]{3,1,2,0:T(8,128)S(1)}, f32[6,20,2,256]{3,1,2,0:T(8,128)S(1)}, u32[]{:S(2)}, u32[]{:S(2)}) collective-permute-start(f32[6,20,2,256]{3,1,2,0:T(8,128)S(1)} %get-tuple-element.125), channel_id=1, source_target_pairs={{1,0},{2,1},{3,2},{4,3},{5,4},{6,5},{7,6},{9,8},{10,9},{11,10},{12... | collective-permute-start | bytes 737288 | tf_op jit(solution)/shard_map/ppermute | solution.py:23
  280.3 8.4 %collective-permute-start.20 = (f32[3,2,16,256]{3,1,2,0:T(2,128)S(1)}, f32[3,2,16,256]{3,1,2,0:T(2,128)S(1)}, u32[]{:S(2)}, u32[]{:S(2)}) collective-permute-start(f32[3,2,16,256]{3,1,2,0:T(2,128)S(1)} %get-tuple-element.152), channel_id=1, source_target_pairs={{0,8},{8,16},{16,24},{24,32},{32,40},{40,48},{48,56},{56,64},{64,7... | collective-permute-start | bytes 294920 | tf_op jit(solution)/shard_map/ppermute | solution.py:22
  282.3 8.2 %collective-permute-start.21 = (f32[3,2,16,256]{3,1,2,0:T(2,128)S(1)}, f32[3,2,16,256]{3,1,2,0:T(2,128)S(1)}, u32[]{:S(2)}, u32[]{:S(2)}) collective-permute-start(f32[3,2,16,256]{3,1,2,0:T(2,128)S(1)} %get-tuple-element.153), channel_id=1, source_target_pairs={{8,0},{16,8},{24,16},{32,24},{40,32},{48,40},{56,48},{64,56},{72,6... | collective-permute-start | bytes 294920 | tf_op jit(solution)/shard_map/ppermute | solution.py:23
  290.6 7.1 %collective-permute-start.22 = (f32[3,20,2,256]{3,1,2,0:T(8,128)S(1)}, f32[3,20,2,256]{3,1,2,0:T(8,128)S(1)}, u32[]{:S(2)}, u32[]{:S(2)}) collective-permute-start(f32[3,20,2,256]{3,1,2,0:T(8,128)S(1)} %get-tuple-element.144), channel_id=1, source_target_pairs={{0,1},{1,2},{2,3},{3,4},{4,5},{5,6},{6,7},{8,9},{9,10},{10,11},{11... | collective-permute-start | bytes 368648 | tf_op jit(solution)/shard_map/ppermute | solution.py:22
  295.0 7.0 %collective-permute-start.23 = (f32[3,20,2,256]{3,1,2,0:T(8,128)S(1)}, f32[3,20,2,256]{3,1,2,0:T(8,128)S(1)}, u32[]{:S(2)}, u32[]{:S(2)}) collective-permute-start(f32[3,20,2,256]{3,1,2,0:T(8,128)S(1)} %get-tuple-element.145), channel_id=1, source_target_pairs={{1,0},{2,1},{3,2},{4,3},{5,4},{6,5},{7,6},{9,8},{10,9},{11,10},{12... | collective-permute-start | bytes 368648 | tf_op jit(solution)/shard_map/ppermute | solution.py:23
  306.8 9.4 %collective-permute-start.24 = (f32[6,2,16,256]{3,1,2,0:T(2,128)S(1)}, f32[6,2,16,256]{3,1,2,0:T(2,128)S(1)}, u32[]{:S(2)}, u32[]{:S(2)}) collective-permute-start(f32[6,2,16,256]{3,1,2,0:T(2,128)S(1)} %get-tuple-element.130), channel_id=1, source_target_pairs={{0,8},{8,16},{16,24},{24,32},{32,40},{40,48},{48,56},{56,64},{64,7... | collective-permute-start | bytes 589832 | tf_op jit(solution)/shard_map/ppermute | solution.py:22
  308.7 9.3 %collective-permute-start.25 = (f32[6,2,16,256]{3,1,2,0:T(2,128)S(1)}, f32[6,2,16,256]{3,1,2,0:T(2,128)S(1)}, u32[]{:S(2)}, u32[]{:S(2)}) collective-permute-start(f32[6,2,16,256]{3,1,2,0:T(2,128)S(1)} %get-tuple-element.131), channel_id=1, source_target_pairs={{8,0},{16,8},{24,16},{32,24},{40,32},{48,40},{56,48},{64,56},{72,6... | collective-permute-start | bytes 589832 | tf_op jit(solution)/shard_map/ppermute | solution.py:23
  318.1 17.7 %collective-permute-start.26 = (f32[6,20,2,256]{3,1,2,0:T(8,128)S(1)}, f32[6,20,2,256]{3,1,2,0:T(8,128)S(1)}, u32[]{:S(2)}, u32[]{:S(2)}) collective-permute-start(f32[6,20,2,256]{3,1,2,0:T(8,128)S(1)} %get-tuple-element.122), channel_id=1, source_target_pairs={{0,1},{1,2},{2,3},{3,4},{4,5},{5,6},{6,7},{8,9},{9,10},{10,11},{11... | collective-permute-start | bytes 737288 | tf_op jit(solution)/shard_map/ppermute | solution.py:22
  322.9 12.9 %collective-permute-start.27 = (f32[6,20,2,256]{3,1,2,0:T(8,128)S(1)}, f32[6,20,2,256]{3,1,2,0:T(8,128)S(1)}, u32[]{:S(2)}, u32[]{:S(2)}) collective-permute-start(f32[6,20,2,256]{3,1,2,0:T(8,128)S(1)} %get-tuple-element.123), channel_id=1, source_target_pairs={{1,0},{2,1},{3,2},{4,3},{5,4},{6,5},{7,6},{9,8},{10,9},{11,10},{12... | collective-permute-start | bytes 737288 | tf_op jit(solution)/shard_map/ppermute | solution.py:23
  342.4 8.4 %collective-permute-start.28 = (f32[3,2,16,256]{3,1,2,0:T(2,128)S(1)}, f32[3,2,16,256]{3,1,2,0:T(2,128)S(1)}, u32[]{:S(2)}, u32[]{:S(2)}) collective-permute-start(f32[3,2,16,256]{3,1,2,0:T(2,128)S(1)} %get-tuple-element.150), channel_id=1, source_target_pairs={{0,8},{8,16},{16,24},{24,32},{32,40},{40,48},{48,56},{56,64},{64,7... | collective-permute-start | bytes 294920 | tf_op jit(solution)/shard_map/ppermute | solution.py:22
  344.3 8.2 %collective-permute-start.29 = (f32[3,2,16,256]{3,1,2,0:T(2,128)S(1)}, f32[3,2,16,256]{3,1,2,0:T(2,128)S(1)}, u32[]{:S(2)}, u32[]{:S(2)}) collective-permute-start(f32[3,2,16,256]{3,1,2,0:T(2,128)S(1)} %get-tuple-element.151), channel_id=1, source_target_pairs={{8,0},{16,8},{24,16},{32,24},{40,32},{48,40},{56,48},{64,56},{72,6... | collective-permute-start | bytes 294920 | tf_op jit(solution)/shard_map/ppermute | solution.py:23
  352.6 7.2 %collective-permute-start.30 = (f32[3,20,2,256]{3,1,2,0:T(8,128)S(1)}, f32[3,20,2,256]{3,1,2,0:T(8,128)S(1)}, u32[]{:S(2)}, u32[]{:S(2)}) collective-permute-start(f32[3,20,2,256]{3,1,2,0:T(8,128)S(1)} %get-tuple-element.142), channel_id=1, source_target_pairs={{0,1},{1,2},{2,3},{3,4},{4,5},{5,6},{6,7},{8,9},{9,10},{10,11},{11... | collective-permute-start | bytes 368648 | tf_op jit(solution)/shard_map/ppermute | solution.py:22
  357.0 7.0 %collective-permute-start.31 = (f32[3,20,2,256]{3,1,2,0:T(8,128)S(1)}, f32[3,20,2,256]{3,1,2,0:T(8,128)S(1)}, u32[]{:S(2)}, u32[]{:S(2)}) collective-permute-start(f32[3,20,2,256]{3,1,2,0:T(8,128)S(1)} %get-tuple-element.143), channel_id=1, source_target_pairs={{1,0},{2,1},{3,2},{4,3},{5,4},{6,5},{7,6},{9,8},{10,9},{11,10},{12... | collective-permute-start | bytes 368648 | tf_op jit(solution)/shard_map/ppermute | solution.py:23
  369.5 90.5 %reduce-scatter.9.cloned.1.call-start = ((), (), s32[]{:S(2)}) async-start(), calls=%async_computation.3 | async-start | bytes 147456
Sparse Core Ops, SparseCore 0:
  369.6 49.5 reduce-scatter.6
  421.9 38.0 reduce-scatter.8
where the time goes:
time: 475 us; the launch traced here: 468 us
  waiting for transfers between devices  170 us (36%)
  blocking collectives  116 us (24%)
  starting transfers between devices  107 us (23%)
  other arithmetic  43.4 us (9%)
  local copies, waits for them, and re-layouts  16 us (3%)
  between operations  15.8 us (3%)
    unnamed x4, waiting for transfers between devices  86.3 us
    ppermute x16, starting transfers between devices, with_halo(): after = lax.ppermute(first, axis, down)  58.7 us
    ppermute x16, waiting for transfers between devices, with_halo(): before = lax.ppermute(last, axis, up)  56.3 us
    ppermute x16, starting transfers between devices, with_halo(): before = lax.ppermute(last, axis, up)  48.1 us
    all_gather x1, blocking collectives, local(): lax.all_gather(prestress, 'cross', axis=1, tiled=True)  31.8 us
    all_gather x1, blocking collectives, local(): lax.all_gather(state, 'cross', axis=1, tiled=True)  28.3 us
    all_gather x1, blocking collectives, local(): lax.all_gather(normal_stress, 'cross', axis=1, tiled=True)  28.2 us
    all_gather x1, blocking collectives, local(): lax.all_gather(rate_a, 'cross', axis=1, tiled=True)  28.2 us
  transfers between devices with their start and end apart: 34, of which 27 were waited for; matrix products, arithmetic and copies ran while one was open for 2% of the time, Pallas kernels for 0%

commit v1 on v0

--- a/solution.py
+++ b/solution.py
@@ -10,6 +10,13 @@
 evolve_rate = 1e-05
 base_friction = 0.6
 evolve_b = 0.03
+
+
+def streams_match(slab_in, lane_axis, dim_no):
+    all_values = jax.lax.all_to_all(
+        jnp.stack([slab_in for _ in range(jax.lax.axis_size(lane_axis))]), lane_axis, 0, 0
+    )
+    return jnp.concatenate(all_values, dim_no)
 
 
 def with_halo(shard, sides, width):
@@ -117,7 +124,7 @@
         lax.all_gather(prestress, "cross", axis=1, tiled=True),
         lax.all_gather(normal_stress, "cross", axis=1, tiled=True),
         lax.all_gather(rate_a, "cross", axis=1, tiled=True),
-        lax.all_gather(state, "cross", axis=1, tiled=True),
+        streams_match(state, "cross", 1),
     )
     slip = jnp.zeros_like(fault_state)
     for iteration in range(STEPS):

time: 475 us -> 454 us (0.956)
  blocking collectives: 116 us -> 85.1 us
  starting transfers between devices: 107 us -> 116 us
    all_gather x1 -> x0, blocking collectives: 28.3 us -> none  [local(): lax.all_gather(state, 'cross', axis=1, tiled=True)]
    all_to_all x0 -> x1, starting transfers between devices: none -> 7.13 us  [streams_match(): jax.lax.all_to_all(jnp.stack([slab_in for _ in range(jax.lax.axis_size(la...]
    unnamed x29 -> x32, local copies, waits for them, and re-layouts: 11.9 us -> 12.6 us
  transfers between devices with their start and end apart: 34 -> 35, of which waited for: 27 -> 27; matrix products, arithmetic and copies ran while one was open for 2% -> 2% of each run, Pallas kernels for 0% -> 0%
where the time goes in v1:
time: 454 us; the launch traced here: 447 us
  waiting for transfers between devices  169 us (37%)
  starting transfers between devices  116 us (26%)
  blocking collectives  85.1 us (19%)
  other arithmetic  45.1 us (10%)
  local copies, waits for them, and re-layouts  16.6 us (4%)
  between operations  15.9 us (4%)
    unnamed x4, waiting for transfers between devices  85.7 us
    ppermute x16, starting transfers between devices, with_halo(): after = lax.ppermute(first, axis, down)  58.7 us
    ppermute x16, waiting for transfers between devices, with_halo(): before = lax.ppermute(last, axis, up)  55.6 us
    ppermute x16, starting transfers between devices, with_halo(): before = lax.ppermute(last, axis, up)  50 us
    all_gather x1, blocking collectives, local(): lax.all_gather(prestress, 'cross', axis=1, tiled=True)  28.7 us
    all_gather x1, blocking collectives, local(): lax.all_gather(rate_a, 'cross', axis=1, tiled=True)  28.3 us
    all_gather x1, blocking collectives, local(): lax.all_gather(normal_stress, 'cross', axis=1, tiled=True)  28.2 us
    ppermute x16, waiting for transfers between devices, with_halo(): after = lax.ppermute(first, axis, down)  27.3 us
  transfers between devices with their start and end apart: 35, of which 27 were waited for; matrix products, arithmetic and copies ran while one was open for 2% of the time, Pallas kernels for 0%

profile of v1, /device:TPU:32, one launch (start us, length us, event | category | flops | bytes accessed | tf_op | source)
XLA Modules:
  0.0 447.2 jit_solution(4799423150497831871)
XLA Ops:
  7.2 2.3 copy.50
  9.7 1.9 collective-permute-start
  11.6 6.0 %collective-permute-start.1 = (f32[6,2,16,256]{3,1,2,0:T(2,128)S(1)}, f32[6,2,16,256]{3,1,2,0:T(2,128)S(1)}, u32[]{:S(2)}, u32[]{:S(2)}) collective-permute-start(f32[6,2,16,256]{3,1,2,0:T(2,128)S(1)} %get-tuple-element.137), channel_id=1, source_target_pairs={{8,0},{16,8},{24,16},{32,24},{40,32},{48,40},{56,48},{64,56},{72,6... | collective-permute-start | bytes 589832 | tf_op jit(solution)/shard_map/ppermute | solution.py:30
  17.6 1.4 collective-permute-done
  19.0 1.8 collective-permute-done.1
  20.9 3.5 collective-permute-start.2
  24.4 1.3 collective-permute-start.3
  25.9 11.5 %collective-permute-done.2 = f32[6,20,2,256]{3,1,2,0:T(8,128)S(1)} collective-permute-done((f32[6,20,2,256]{3,1,2,0:T(8,128)S(1)}, f32[6,20,2,256]{3,1,2,0:T(8,128)S(1)}, u32[]{:S(2)}, u32[]{:S(2)}) %collective-permute-start.2) | collective-permute-done | bytes 245792 | tf_op jit(solution)/shard_map/ppermute | solution.py:29
  37.4 3.0 select_maximum_fusion.12
  44.1 2.7 collective-permute-start.4
  46.8 5.3 %collective-permute-start.5 = (f32[3,2,16,256]{3,1,2,0:T(2,128)S(1)}, f32[3,2,16,256]{3,1,2,0:T(2,128)S(1)}, u32[]{:S(2)}, u32[]{:S(2)}) collective-permute-start(f32[3,2,16,256]{3,1,2,0:T(2,128)S(1)} %get-tuple-element.157), channel_id=1, source_target_pairs={{8,0},{16,8},{24,16},{32,24},{40,32},{48,40},{56,48},{64,56},{72,6... | collective-permute-start | bytes 294920 | tf_op jit(solution)/shard_map/ppermute | solution.py:30
  52.4 1.8 collective-permute-done.5
  54.3 5.0 %collective-permute-start.6 = (f32[3,20,2,256]{3,1,2,0:T(8,128)S(1)}, f32[3,20,2,256]{3,1,2,0:T(8,128)}, u32[]{:S(2)}, u32[]{:S(2)}) collective-permute-start(f32[3,20,2,256]{3,1,2,0:T(8,128)S(1)} %get-tuple-element.148), channel_id=1, source_target_pairs={{0,1},{1,2},{2,3},{3,4},{4,5},{5,6},{6,7},{8,9},{9,10},{10,11},{11... | collective-permute-start | bytes 368648 | tf_op jit(solution)/shard_map/ppermute | solution.py:29
  61.4 7.1 %all-to-all-start = ((f32[8,1,512]{2,1,0:T(1,128)}), f32[8,1,512]{2,1,0:T(1,128)S(1)}, u32[]{:S(2)}, u32[]{:S(2)}) async-start(f32[8,1,512]{2,1,0:T(1,128)} %reshape.185), calls=%async_computation | async-start | bytes 32768 | tf_op jit(solution)/shard_map/all_to_all | solution.py:16
  68.6 28.7 %all-gather = f32[8,32,16]{1,2,0:T(8,128)S(1)} all-gather(f32[1,32,16]{1,2,0:T(8,128)S(1)} %bitcast.290), channel_id=1, replica_groups=mesh['strike'=32,'cross'=8] {'cross'}, dimensions={0}, use_global_device_ids=true | all-gather | bytes 18432 | tf_op jit(solution)/shard_map/all_gather | solution.py:124
  97.4 28.2 %all-gather.2 = f32[8,32,16]{1,2,0:T(8,128)S(1)} all-gather(f32[1,32,16]{1,2,0:T(8,128)S(1)} %bitcast.291), channel_id=1, replica_groups=mesh['strike'=32,'cross'=8] {'cross'}, dimensions={0}, use_global_device_ids=true | all-gather | bytes 18432 | tf_op jit(solution)/shard_map/all_gather | solution.py:125
  125.6 28.3 %all-gather.1 = f32[8,32,16]{1,2,0:T(8,128)S(1)} all-gather(f32[1,32,16]{1,2,0:T(8,128)S(1)} %bitcast.292), channel_id=1, replica_groups=mesh['strike'=32,'cross'=8] {'cross'}, dimensions={0}, use_global_device_ids=true | all-gather | bytes 18432 | tf_op jit(solution)/shard_map/all_gather | solution.py:126
  156.7 2.0 select_maximum_fusion.28
  164.5 1.9 collective-permute-start.8
  166.4 6.0 %collective-permute-start.9 = (f32[6,2,16,256]{3,1,2,0:T(2,128)S(1)}, f32[6,2,16,256]{3,1,2,0:T(2,128)S(1)}, u32[]{:S(2)}, u32[]{:S(2)}) collective-permute-start(f32[6,2,16,256]{3,1,2,0:T(2,128)S(1)} %get-tuple-element.135), channel_id=1, source_target_pairs={{8,0},{16,8},{24,16},{32,24},{40,32},{48,40},{56,48},{64,56},{72,6... | collective-permute-start | bytes 589832 | tf_op jit(solution)/shard_map/ppermute | solution.py:30
  172.5 1.4 collective-permute-done.8
  173.9 1.8 collective-permute-done.9
  175.8 3.4 collective-permute-start.10
  180.4 11.6 %collective-permute-done.10 = f32[6,20,2,256]{3,1,2,0:T(8,128)S(1)} collective-permute-done((f32[6,20,2,256]{3,1,2,0:T(8,128)S(1)}, f32[6,20,2,256]{3,1,2,0:T(8,128)S(1)}, u32[]{:S(2)}, u32[]{:S(2)}) %collective-permute-start.10) | collective-permute-done | bytes 245792 | tf_op jit(solution)/shard_map/ppermute | solution.py:29
  192.0 3.0 select_maximum_fusion.8
  198.5 1.9 collective-permute-start.12
  200.5 6.0 %collective-permute-start.13 = (f32[3,2,16,256]{3,1,2,0:T(2,128)S(1)}, f32[3,2,16,256]{3,1,2,0:T(2,128)S(1)}, u32[]{:S(2)}, u32[]{:S(2)}) collective-permute-start(f32[3,2,16,256]{3,1,2,0:T(2,128)S(1)} %get-tuple-element.155), channel_id=1, source_target_pairs={{8,0},{16,8},{24,16},{32,24},{40,32},{48,40},{56,48},{64,56},{72,6... | collective-permute-start | bytes 294920 | tf_op jit(solution)/shard_map/ppermute | solution.py:30
  206.9 1.8 collective-permute-done.13
  208.8 4.4 collective-permute-start.14
  213.2 1.5 collective-permute-start.15
  215.8 4.4 collective-permute-done.15
  225.0 1.9 collective-permute-start.16
  226.9 6.0 %collective-permute-start.17 = (f32[6,2,16,256]{3,1,2,0:T(2,128)S(1)}, f32[6,2,16,256]{3,1,2,0:T(2,128)S(1)}, u32[]{:S(2)}, u32[]{:S(2)}) collective-permute-start(f32[6,2,16,256]{3,1,2,0:T(2,128)S(1)} %get-tuple-element.133), channel_id=1, source_target_pairs={{8,0},{16,8},{24,16},{32,24},{40,32},{48,40},{56,48},{64,56},{72,6... | collective-permute-start | bytes 589832 | tf_op jit(solution)/shard_map/ppermute | solution.py:30
  233.0 1.4 collective-permute-done.16
  234.4 1.8 collective-permute-done.17
  236.3 4.0 collective-permute-start.18
  240.3 1.3 collective-permute-start.19
  241.6 11.6 %collective-permute-done.18 = f32[6,20,2,256]{3,1,2,0:T(8,128)S(1)} collective-permute-done((f32[6,20,2,256]{3,1,2,0:T(8,128)S(1)}, f32[6,20,2,256]{3,1,2,0:T(8,128)S(1)}, u32[]{:S(2)}, u32[]{:S(2)}) %collective-permute-start.18) | collective-permute-done | bytes 245792 | tf_op jit(solution)/shard_map/ppermute | solution.py:29
  253.1 3.0 select_maximum_fusion.4
  259.7 1.9 collective-permute-start.20
  261.6 6.0 %collective-permute-start.21 = (f32[3,2,16,256]{3,1,2,0:T(2,128)S(1)}, f32[3,2,16,256]{3,1,2,0:T(2,128)S(1)}, u32[]{:S(2)}, u32[]{:S(2)}) collective-permute-start(f32[3,2,16,256]{3,1,2,0:T(2,128)S(1)} %get-tuple-element.153), channel_id=1, source_target_pairs={{8,0},{16,8},{24,16},{32,24},{40,32},{48,40},{56,48},{64,56},{72,6... | collective-permute-start | bytes 294920 | tf_op jit(solution)/shard_map/ppermute | solution.py:30
  268.1 1.8 collective-permute-done.21
  269.9 4.4 collective-permute-start.22
  274.3 1.7 collective-permute-start.23
  276.9 4.4 collective-permute-done.23
  286.1 1.9 collective-permute-start.24
  288.1 6.0 %collective-permute-start.25 = (f32[6,2,16,256]{3,1,2,0:T(2,128)S(1)}, f32[6,2,16,256]{3,1,2,0:T(2,128)S(1)}, u32[]{:S(2)}, u32[]{:S(2)}) collective-permute-start(f32[6,2,16,256]{3,1,2,0:T(2,128)S(1)} %get-tuple-element.131), channel_id=1, source_target_pairs={{8,0},{16,8},{24,16},{32,24},{40,32},{48,40},{56,48},{64,56},{72,6... | collective-permute-start | bytes 589832 | tf_op jit(solution)/shard_map/ppermute | solution.py:30
  294.1 1.4 collective-permute-done.24
  295.5 1.8 collective-permute-done.25
  297.4 4.8 %collective-permute-start.26 = (f32[6,20,2,256]{3,1,2,0:T(8,128)S(1)}, f32[6,20,2,256]{3,1,2,0:T(8,128)S(1)}, u32[]{:S(2)}, u32[]{:S(2)}) collective-permute-start(f32[6,20,2,256]{3,1,2,0:T(8,128)S(1)} %get-tuple-element.122), channel_id=1, source_target_pairs={{0,1},{1,2},{2,3},{3,4},{4,5},{5,6},{6,7},{8,9},{9,10},{10,11},{11... | collective-permute-start | bytes 737288 | tf_op jit(solution)/shard_map/ppermute | solution.py:29
  303.5 11.6 %collective-permute-done.26 = f32[6,20,2,256]{3,1,2,0:T(8,128)S(1)} collective-permute-done((f32[6,20,2,256]{3,1,2,0:T(8,128)S(1)}, f32[6,20,2,256]{3,1,2,0:T(8,128)S(1)}, u32[]{:S(2)}, u32[]{:S(2)}) %collective-permute-start.26) | collective-permute-done | bytes 245792 | tf_op jit(solution)/shard_map/ppermute | solution.py:29
  315.1 3.0 select_maximum_fusion
  321.8 1.9 collective-permute-start.28
  323.7 6.0 %collective-permute-start.29 = (f32[3,2,16,256]{3,1,2,0:T(2,128)S(1)}, f32[3,2,16,256]{3,1,2,0:T(2,128)S(1)}, u32[]{:S(2)}, u32[]{:S(2)}) collective-permute-start(f32[3,2,16,256]{3,1,2,0:T(2,128)S(1)} %get-tuple-element.151), channel_id=1, source_target_pairs={{8,0},{16,8},{24,16},{32,24},{40,32},{48,40},{56,48},{64,56},{72,6... | collective-permute-start | bytes 294920 | tf_op jit(solution)/shard_map/ppermute | solution.py:30
  330.2 1.8 collective-permute-done.29
  332.0 4.4 collective-permute-start.30
  336.4 1.5 collective-permute-start.31
  337.9 1.3 copy.67
  339.2 4.2 collective-permute-done.31
  349.7 2.0 copy.68
  351.7 46.3 %reduce-scatter.7.cloned.1.call-done = f32[32,16]{1,0:T(8,128)} async-done(((f32[256,16]{1,0:T(8,128)}), f32[32,16]{1,0:T(8,128)}) %reduce-scatter.7.cloned.1.call-update) | async-done | bytes 2064
  398.1 1.4 copy.70
  399.5 39.4 %reduce-scatter.9.cloned.1.call-done = f32[32,16]{1,0:T(8,128)} async-done(((f32[256,16]{1,0:T(8,128)}), f32[32,16]{1,0:T(8,128)}) %reduce-scatter.9.cloned.1.call-update) | async-done | bytes 2064
  438.8 1.4 copy.72
  (140 shorter events, 47.1 us)
Async XLA Ops:
  9.5 16.2 %copy-start.4 = (f32[16,16,256]{2,1,0:T(8,128)S(1)}, f32[16,16,256]{2,1,0:T(8,128)}, u32[]{:S(2)}) copy-start(f32[16,16,256]{2,1,0:T(8,128)} %param.20) | copy-start | bytes 786436
  9.7 9.4 %collective-permute-start = (f32[6,2,16,256]{3,1,2,0:T(2,128)S(1)}, f32[6,2,16,256]{3,1,2,0:T(2,128)S(1)}, u32[]{:S(2)}, u32[]{:S(2)}) collective-permute-start(f32[6,2,16,256]{3,1,2,0:T(2,128)S(1)} %get-tuple-element.136), channel_id=1, source_target_pairs={{0,8},{8,16},{16,24},{24,32},{32,40},{40,48},{48,56},{56,64},{64,7... | collective-permute-start | bytes 589832 | tf_op jit(solution)/shard_map/ppermute | solution.py:29
  11.6 9.2 %collective-permute-start.1 = (f32[6,2,16,256]{3,1,2,0:T(2,128)S(1)}, f32[6,2,16,256]{3,1,2,0:T(2,128)S(1)}, u32[]{:S(2)}, u32[]{:S(2)}) collective-permute-start(f32[6,2,16,256]{3,1,2,0:T(2,128)S(1)} %get-tuple-element.137), channel_id=1, source_target_pairs={{8,0},{16,8},{24,16},{32,24},{40,32},{48,40},{56,48},{64,56},{72,6... | collective-permute-start | bytes 589832 | tf_op jit(solution)/shard_map/ppermute | solution.py:30
  20.9 16.5 %collective-permute-start.2 = (f32[6,20,2,256]{3,1,2,0:T(8,128)S(1)}, f32[6,20,2,256]{3,1,2,0:T(8,128)S(1)}, u32[]{:S(2)}, u32[]{:S(2)}) collective-permute-start(f32[6,20,2,256]{3,1,2,0:T(8,128)S(1)} %get-tuple-element.128), channel_id=1, source_target_pairs={{0,1},{1,2},{2,3},{3,4},{4,5},{5,6},{6,7},{8,9},{9,10},{10,11},{11... | collective-permute-start | bytes 737288 | tf_op jit(solution)/shard_map/ppermute | solution.py:29
  24.4 13.0 %collective-permute-start.3 = (f32[6,20,2,256]{3,1,2,0:T(8,128)S(1)}, f32[6,20,2,256]{3,1,2,0:T(8,128)S(1)}, u32[]{:S(2)}, u32[]{:S(2)}) collective-permute-start(f32[6,20,2,256]{3,1,2,0:T(8,128)S(1)} %get-tuple-element.129), channel_id=1, source_target_pairs={{1,0},{2,1},{3,2},{4,3},{5,4},{6,5},{7,6},{9,8},{10,9},{11,10},{12... | collective-permute-start | bytes 737288 | tf_op jit(solution)/shard_map/ppermute | solution.py:30
  42.3 1.1 copy-start.1
  43.5 17.2 %copy-start.5 = (f32[16,32]{1,0:T(8,128)S(1)}, f32[16,32]{1,0:T(8,128)}, u32[]{:S(2)}) copy-start(f32[16,32]{1,0:T(8,128)} %param.27) | copy-start | bytes 6148
  43.5 25.1 %copy-start.6 = (f32[16,32]{1,0:T(8,128)S(1)}, f32[16,32]{1,0:T(8,128)}, u32[]{:S(2)}) copy-start(f32[16,32]{1,0:T(8,128)} %param.24) | copy-start | bytes 6148
  43.5 53.9 %copy-start.7 = (f32[16,32]{1,0:T(8,128)S(1)}, f32[16,32]{1,0:T(8,128)}, u32[]{:S(2)}) copy-start(f32[16,32]{1,0:T(8,128)} %param.25) | copy-start | bytes 6148
  43.5 82.2 %copy-start.8 = (f32[16,32]{1,0:T(8,128)S(1)}, f32[16,32]{1,0:T(8,128)}, u32[]{:S(2)}) copy-start(f32[16,32]{1,0:T(8,128)} %param.26) | copy-start | bytes 6148
  43.5 110.6 %copy-start.9 = (s32[32]{0:T(128)S(1)}, s32[32]{0:T(128)}, u32[]{:S(2)}) copy-start(s32[32]{0:T(128)} %param.23) | copy-start | bytes 388
  44.1 8.3 %collective-permute-start.4 = (f32[3,2,16,256]{3,1,2,0:T(2,128)S(1)}, f32[3,2,16,256]{3,1,2,0:T(2,128)S(1)}, u32[]{:S(2)}, u32[]{:S(2)}) collective-permute-start(f32[3,2,16,256]{3,1,2,0:T(2,128)S(1)} %get-tuple-element.156), channel_id=1, source_target_pairs={{0,8},{8,16},{16,24},{24,32},{32,40},{40,48},{48,56},{56,64},{64,7... | collective-permute-start | bytes 294920 | tf_op jit(solution)/shard_map/ppermute | solution.py:29
  46.8 7.5 %collective-permute-start.5 = (f32[3,2,16,256]{3,1,2,0:T(2,128)S(1)}, f32[3,2,16,256]{3,1,2,0:T(2,128)S(1)}, u32[]{:S(2)}, u32[]{:S(2)}) collective-permute-start(f32[3,2,16,256]{3,1,2,0:T(2,128)S(1)} %get-tuple-element.157), channel_id=1, source_target_pairs={{8,0},{16,8},{24,16},{32,24},{40,32},{48,40},{56,48},{64,56},{72,6... | collective-permute-start | bytes 294920 | tf_op jit(solution)/shard_map/ppermute | solution.py:30
  54.3 102.4 %collective-permute-start.6 = (f32[3,20,2,256]{3,1,2,0:T(8,128)S(1)}, f32[3,20,2,256]{3,1,2,0:T(8,128)}, u32[]{:S(2)}, u32[]{:S(2)}) collective-permute-start(f32[3,20,2,256]{3,1,2,0:T(8,128)S(1)} %get-tuple-element.148), channel_id=1, source_target_pairs={{0,1},{1,2},{2,3},{3,4},{4,5},{5,6},{6,7},{8,9},{9,10},{10,11},{11... | collective-permute-start | bytes 368648 | tf_op jit(solution)/shard_map/ppermute | solution.py:29
  59.4 97.4 %collective-permute-start.7 = (f32[3,20,2,256]{3,1,2,0:T(8,128)S(1)}, f32[3,20,2,256]{3,1,2,0:T(8,128)}, u32[]{:S(2)}, u32[]{:S(2)}) collective-permute-start(f32[3,20,2,256]{3,1,2,0:T(8,128)S(1)} %get-tuple-element.149), channel_id=1, source_target_pairs={{1,0},{2,1},{3,2},{4,3},{5,4},{6,5},{7,6},{9,8},{10,9},{11,10},{12... | collective-permute-start | bytes 368648 | tf_op jit(solution)/shard_map/ppermute | solution.py:30
  61.4 94.0 %all-to-all-start = ((f32[8,1,512]{2,1,0:T(1,128)}), f32[8,1,512]{2,1,0:T(1,128)S(1)}, u32[]{:S(2)}, u32[]{:S(2)}) async-start(f32[8,1,512]{2,1,0:T(1,128)} %reshape.185), calls=%async_computation | async-start | bytes 32768 | tf_op jit(solution)/shard_map/all_to_all | solution.py:16
  68.5 329.6 %reduce-scatter.7.cloned.1.call-start = ((), (), s32[]{:S(2)}) async-start(), calls=%async_computation.3 | async-start | bytes 147456
  159.5 1.0 copy-start
  159.6 1.0 copy-start.3
  161.5 1.4 copy-start.2
  164.5 9.4 %collective-permute-start.8 = (f32[6,2,16,256]{3,1,2,0:T(2,128)S(1)}, f32[6,2,16,256]{3,1,2,0:T(2,128)S(1)}, u32[]{:S(2)}, u32[]{:S(2)}) collective-permute-start(f32[6,2,16,256]{3,1,2,0:T(2,128)S(1)} %get-tuple-element.134), channel_id=1, source_target_pairs={{0,8},{8,16},{16,24},{24,32},{32,40},{40,48},{48,56},{56,64},{64,7... | collective-permute-start | bytes 589832 | tf_op jit(solution)/shard_map/ppermute | solution.py:29
  166.4 9.3 %collective-permute-start.9 = (f32[6,2,16,256]{3,1,2,0:T(2,128)S(1)}, f32[6,2,16,256]{3,1,2,0:T(2,128)S(1)}, u32[]{:S(2)}, u32[]{:S(2)}) collective-permute-start(f32[6,2,16,256]{3,1,2,0:T(2,128)S(1)} %get-tuple-element.135), channel_id=1, source_target_pairs={{8,0},{16,8},{24,16},{32,24},{40,32},{48,40},{56,48},{64,56},{72,6... | collective-permute-start | bytes 589832 | tf_op jit(solution)/shard_map/ppermute | solution.py:30
  175.8 16.2 %collective-permute-start.10 = (f32[6,20,2,256]{3,1,2,0:T(8,128)S(1)}, f32[6,20,2,256]{3,1,2,0:T(8,128)S(1)}, u32[]{:S(2)}, u32[]{:S(2)}) collective-permute-start(f32[6,20,2,256]{3,1,2,0:T(8,128)S(1)} %get-tuple-element.126), channel_id=1, source_target_pairs={{0,1},{1,2},{2,3},{3,4},{4,5},{5,6},{6,7},{8,9},{9,10},{10,11},{11... | collective-permute-start | bytes 737288 | tf_op jit(solution)/shard_map/ppermute | solution.py:29
  179.1 12.9 %collective-permute-start.11 = (f32[6,20,2,256]{3,1,2,0:T(8,128)S(1)}, f32[6,20,2,256]{3,1,2,0:T(8,128)S(1)}, u32[]{:S(2)}, u32[]{:S(2)}) collective-permute-start(f32[6,20,2,256]{3,1,2,0:T(8,128)S(1)} %get-tuple-element.127), channel_id=1, source_target_pairs={{1,0},{2,1},{3,2},{4,3},{5,4},{6,5},{7,6},{9,8},{10,9},{11,10},{12... | collective-permute-start | bytes 737288 | tf_op jit(solution)/shard_map/ppermute | solution.py:30
  198.5 8.4 %collective-permute-start.12 = (f32[3,2,16,256]{3,1,2,0:T(2,128)S(1)}, f32[3,2,16,256]{3,1,2,0:T(2,128)S(1)}, u32[]{:S(2)}, u32[]{:S(2)}) collective-permute-start(f32[3,2,16,256]{3,1,2,0:T(2,128)S(1)} %get-tuple-element.154), channel_id=1, source_target_pairs={{0,8},{8,16},{16,24},{24,32},{32,40},{40,48},{48,56},{56,64},{64,7... | collective-permute-start | bytes 294920 | tf_op jit(solution)/shard_map/ppermute | solution.py:29
  200.5 8.2 %collective-permute-start.13 = (f32[3,2,16,256]{3,1,2,0:T(2,128)S(1)}, f32[3,2,16,256]{3,1,2,0:T(2,128)S(1)}, u32[]{:S(2)}, u32[]{:S(2)}) collective-permute-start(f32[3,2,16,256]{3,1,2,0:T(2,128)S(1)} %get-tuple-element.155), channel_id=1, source_target_pairs={{8,0},{16,8},{24,16},{32,24},{40,32},{48,40},{56,48},{64,56},{72,6... | collective-permute-start | bytes 294920 | tf_op jit(solution)/shard_map/ppermute | solution.py:30
  208.8 7.1 %collective-permute-start.14 = (f32[3,20,2,256]{3,1,2,0:T(8,128)S(1)}, f32[3,20,2,256]{3,1,2,0:T(8,128)S(1)}, u32[]{:S(2)}, u32[]{:S(2)}) collective-permute-start(f32[3,20,2,256]{3,1,2,0:T(8,128)S(1)} %get-tuple-element.146), channel_id=1, source_target_pairs={{0,1},{1,2},{2,3},{3,4},{4,5},{5,6},{6,7},{8,9},{9,10},{10,11},{11... | collective-permute-start | bytes 368648 | tf_op jit(solution)/shard_map/ppermute | solution.py:29
  213.2 7.0 %collective-permute-start.15 = (f32[3,20,2,256]{3,1,2,0:T(8,128)S(1)}, f32[3,20,2,256]{3,1,2,0:T(8,128)S(1)}, u32[]{:S(2)}, u32[]{:S(2)}) collective-permute-start(f32[3,20,2,256]{3,1,2,0:T(8,128)S(1)} %get-tuple-element.147), channel_id=1, source_target_pairs={{1,0},{2,1},{3,2},{4,3},{5,4},{6,5},{7,6},{9,8},{10,9},{11,10},{12... | collective-permute-start | bytes 368648 | tf_op jit(solution)/shard_map/ppermute | solution.py:30
  225.0 9.4 %collective-permute-start.16 = (f32[6,2,16,256]{3,1,2,0:T(2,128)S(1)}, f32[6,2,16,256]{3,1,2,0:T(2,128)S(1)}, u32[]{:S(2)}, u32[]{:S(2)}) collective-permute-start(f32[6,2,16,256]{3,1,2,0:T(2,128)S(1)} %get-tuple-element.132), channel_id=1, source_target_pairs={{0,8},{8,16},{16,24},{24,32},{32,40},{40,48},{48,56},{56,64},{64,7... | collective-permute-start | bytes 589832 | tf_op jit(solution)/shard_map/ppermute | solution.py:29
  226.9 9.3 %collective-permute-start.17 = (f32[6,2,16,256]{3,1,2,0:T(2,128)S(1)}, f32[6,2,16,256]{3,1,2,0:T(2,128)S(1)}, u32[]{:S(2)}, u32[]{:S(2)}) collective-permute-start(f32[6,2,16,256]{3,1,2,0:T(2,128)S(1)} %get-tuple-element.133), channel_id=1, source_target_pairs={{8,0},{16,8},{24,16},{32,24},{40,32},{48,40},{56,48},{64,56},{72,6... | collective-permute-start | bytes 589832 | tf_op jit(solution)/shard_map/ppermute | solution.py:30
  236.3 16.9 %collective-permute-start.18 = (f32[6,20,2,256]{3,1,2,0:T(8,128)S(1)}, f32[6,20,2,256]{3,1,2,0:T(8,128)S(1)}, u32[]{:S(2)}, u32[]{:S(2)}) collective-permute-start(f32[6,20,2,256]{3,1,2,0:T(8,128)S(1)} %get-tuple-element.124), channel_id=1, source_target_pairs={{0,1},{1,2},{2,3},{3,4},{4,5},{5,6},{6,7},{8,9},{9,10},{10,11},{11... | collective-permute-start | bytes 737288 | tf_op jit(solution)/shard_map/ppermute | solution.py:29
  240.3 12.9 %collective-permute-start.19 = (f32[6,20,2,256]{3,1,2,0:T(8,128)S(1)}, f32[6,20,2,256]{3,1,2,0:T(8,128)S(1)}, u32[]{:S(2)}, u32[]{:S(2)}) collective-permute-start(f32[6,20,2,256]{3,1,2,0:T(8,128)S(1)} %get-tuple-element.125), channel_id=1, source_target_pairs={{1,0},{2,1},{3,2},{4,3},{5,4},{6,5},{7,6},{9,8},{10,9},{11,10},{12... | collective-permute-start | bytes 737288 | tf_op jit(solution)/shard_map/ppermute | solution.py:30
  259.7 8.4 %collective-permute-start.20 = (f32[3,2,16,256]{3,1,2,0:T(2,128)S(1)}, f32[3,2,16,256]{3,1,2,0:T(2,128)S(1)}, u32[]{:S(2)}, u32[]{:S(2)}) collective-permute-start(f32[3,2,16,256]{3,1,2,0:T(2,128)S(1)} %get-tuple-element.152), channel_id=1, source_target_pairs={{0,8},{8,16},{16,24},{24,32},{32,40},{40,48},{48,56},{56,64},{64,7... | collective-permute-start | bytes 294920 | tf_op jit(solution)/shard_map/ppermute | solution.py:29
  261.6 8.2 %collective-permute-start.21 = (f32[3,2,16,256]{3,1,2,0:T(2,128)S(1)}, f32[3,2,16,256]{3,1,2,0:T(2,128)S(1)}, u32[]{:S(2)}, u32[]{:S(2)}) collective-permute-start(f32[3,2,16,256]{3,1,2,0:T(2,128)S(1)} %get-tuple-element.153), channel_id=1, source_target_pairs={{8,0},{16,8},{24,16},{32,24},{40,32},{48,40},{56,48},{64,56},{72,6... | collective-permute-start | bytes 294920 | tf_op jit(solution)/shard_map/ppermute | solution.py:30
  269.9 7.1 %collective-permute-start.22 = (f32[3,20,2,256]{3,1,2,0:T(8,128)S(1)}, f32[3,20,2,256]{3,1,2,0:T(8,128)S(1)}, u32[]{:S(2)}, u32[]{:S(2)}) collective-permute-start(f32[3,20,2,256]{3,1,2,0:T(8,128)S(1)} %get-tuple-element.144), channel_id=1, source_target_pairs={{0,1},{1,2},{2,3},{3,4},{4,5},{5,6},{6,7},{8,9},{9,10},{10,11},{11... | collective-permute-start | bytes 368648 | tf_op jit(solution)/shard_map/ppermute | solution.py:29
  274.3 7.0 %collective-permute-start.23 = (f32[3,20,2,256]{3,1,2,0:T(8,128)S(1)}, f32[3,20,2,256]{3,1,2,0:T(8,128)S(1)}, u32[]{:S(2)}, u32[]{:S(2)}) collective-permute-start(f32[3,20,2,256]{3,1,2,0:T(8,128)S(1)} %get-tuple-element.145), channel_id=1, source_target_pairs={{1,0},{2,1},{3,2},{4,3},{5,4},{6,5},{7,6},{9,8},{10,9},{11,10},{12... | collective-permute-start | bytes 368648 | tf_op jit(solution)/shard_map/ppermute | solution.py:30
  286.1 9.4 %collective-permute-start.24 = (f32[6,2,16,256]{3,1,2,0:T(2,128)S(1)}, f32[6,2,16,256]{3,1,2,0:T(2,128)S(1)}, u32[]{:S(2)}, u32[]{:S(2)}) collective-permute-start(f32[6,2,16,256]{3,1,2,0:T(2,128)S(1)} %get-tuple-element.130), channel_id=1, source_target_pairs={{0,8},{8,16},{16,24},{24,32},{32,40},{40,48},{48,56},{56,64},{64,7... | collective-permute-start | bytes 589832 | tf_op jit(solution)/shard_map/ppermute | solution.py:29
  288.1 9.3 %collective-permute-start.25 = (f32[6,2,16,256]{3,1,2,0:T(2,128)S(1)}, f32[6,2,16,256]{3,1,2,0:T(2,128)S(1)}, u32[]{:S(2)}, u32[]{:S(2)}) collective-permute-start(f32[6,2,16,256]{3,1,2,0:T(2,128)S(1)} %get-tuple-element.131), channel_id=1, source_target_pairs={{8,0},{16,8},{24,16},{32,24},{40,32},{48,40},{56,48},{64,56},{72,6... | collective-permute-start | bytes 589832 | tf_op jit(solution)/shard_map/ppermute | solution.py:30
  297.4 17.7 %collective-permute-start.26 = (f32[6,20,2,256]{3,1,2,0:T(8,128)S(1)}, f32[6,20,2,256]{3,1,2,0:T(8,128)S(1)}, u32[]{:S(2)}, u32[]{:S(2)}) collective-permute-start(f32[6,20,2,256]{3,1,2,0:T(8,128)S(1)} %get-tuple-element.122), channel_id=1, source_target_pairs={{0,1},{1,2},{2,3},{3,4},{4,5},{5,6},{6,7},{8,9},{9,10},{10,11},{11... | collective-permute-start | bytes 737288 | tf_op jit(solution)/shard_map/ppermute | solution.py:29
  302.2 12.9 %collective-permute-start.27 = (f32[6,20,2,256]{3,1,2,0:T(8,128)S(1)}, f32[6,20,2,256]{3,1,2,0:T(8,128)S(1)}, u32[]{:S(2)}, u32[]{:S(2)}) collective-permute-start(f32[6,20,2,256]{3,1,2,0:T(8,128)S(1)} %get-tuple-element.123), channel_id=1, source_target_pairs={{1,0},{2,1},{3,2},{4,3},{5,4},{6,5},{7,6},{9,8},{10,9},{11,10},{12... | collective-permute-start | bytes 737288 | tf_op jit(solution)/shard_map/ppermute | solution.py:30
  321.8 8.4 %collective-permute-start.28 = (f32[3,2,16,256]{3,1,2,0:T(2,128)S(1)}, f32[3,2,16,256]{3,1,2,0:T(2,128)S(1)}, u32[]{:S(2)}, u32[]{:S(2)}) collective-permute-start(f32[3,2,16,256]{3,1,2,0:T(2,128)S(1)} %get-tuple-element.150), channel_id=1, source_target_pairs={{0,8},{8,16},{16,24},{24,32},{32,40},{40,48},{48,56},{56,64},{64,7... | collective-permute-start | bytes 294920 | tf_op jit(solution)/shard_map/ppermute | solution.py:29
  323.7 8.2 %collective-permute-start.29 = (f32[3,2,16,256]{3,1,2,0:T(2,128)S(1)}, f32[3,2,16,256]{3,1,2,0:T(2,128)S(1)}, u32[]{:S(2)}, u32[]{:S(2)}) collective-permute-start(f32[3,2,16,256]{3,1,2,0:T(2,128)S(1)} %get-tuple-element.151), channel_id=1, source_target_pairs={{8,0},{16,8},{24,16},{32,24},{40,32},{48,40},{56,48},{64,56},{72,6... | collective-permute-start | bytes 294920 | tf_op jit(solution)/shard_map/ppermute | solution.py:30
  332.0 7.2 %collective-permute-start.30 = (f32[3,20,2,256]{3,1,2,0:T(8,128)S(1)}, f32[3,20,2,256]{3,1,2,0:T(8,128)S(1)}, u32[]{:S(2)}, u32[]{:S(2)}) collective-permute-start(f32[3,20,2,256]{3,1,2,0:T(8,128)S(1)} %get-tuple-element.142), channel_id=1, source_target_pairs={{0,1},{1,2},{2,3},{3,4},{4,5},{5,6},{6,7},{8,9},{9,10},{10,11},{11... | collective-permute-start | bytes 368648 | tf_op jit(solution)/shard_map/ppermute | solution.py:29
  336.4 7.0 %collective-permute-start.31 = (f32[3,20,2,256]{3,1,2,0:T(8,128)S(1)}, f32[3,20,2,256]{3,1,2,0:T(8,128)S(1)}, u32[]{:S(2)}, u32[]{:S(2)}) collective-permute-start(f32[3,20,2,256]{3,1,2,0:T(8,128)S(1)} %get-tuple-element.143), channel_id=1, source_target_pairs={{1,0},{2,1},{3,2},{4,3},{5,4},{6,5},{7,6},{9,8},{10,9},{11,10},{12... | collective-permute-start | bytes 368648 | tf_op jit(solution)/shard_map/ppermute | solution.py:30
  348.8 90.0 %reduce-scatter.9.cloned.1.call-start = ((), (), s32[]{:S(2)}) async-start(), calls=%async_computation.4 | async-start | bytes 147456
Sparse Core Ops, SparseCore 0:
  348.9 49.0 reduce-scatter.6
  400.7 38.0 reduce-scatter.8
